TPU v7x, 128 devices: a whole 4x4x4 slice. The times are simulated.
128 devices in a mesh: ha: 8 (over y_hi, z), wa: 16 (over x, y_lo, core).
Axes of the slice: x: 4, y: 4 (y_hi: 2, y_lo: 2; y = y_hi * 2 + y_lo), z: 4, core: 2. Of those that a mesh axis runs over, the one named last changes fastest.
Arguments:
- latent: bfloat16 [16, 64, 128, 1152], P(None, 'ha', 'wa'), may hold values from -6 to 6
- qkv_weight: bfloat16 [2, 1152, 3456], replicated, as said below
- proj_weight: bfloat16 [2, 1152, 1152], P(None, None, 'wa'), may hold values from -0.1875 to 0.1875
- modulation: float32 [2, 3, 1152], replicated, may hold values from -3 to 3
- regions: int32 [16, 64, 128], P(None, 'ha', 'wa'), may hold values from 0 to 2
- frame_shift: int32 [1], replicated, may hold values from 1 to 7
Outputs:
- result: bfloat16 [16, 64, 128, 1152], P(None, 'ha', 'wa')
Inputs may be any that keep to these rules, and one draw needn't show every extreme that they name: `qkv_weight`: query, key and value projections, scaled by the inverse square root of 1152.
All inputs are finite; a program needn't handle non-finite values.
Results may differ from a plain program's by a relative error of at most 0.0055.
Values may be sent and summed in bfloat16 or wider, within the bound.
A program may use at most 192 MiB of HBM per device.

v0:
```python
import functools
import math

import jax
import jax.numpy as jnp
from jax import lax
from jax.experimental import pallas as pl
from jax.experimental.pallas import tpu as pltpu
from jax.sharding import PartitionSpec as P

D = 1152
HEADS = 16
HD = 72
BIG = 1e30
SCALE = math.log2(math.e) / math.sqrt(HD)
F32 = jnp.float32
BF16 = jnp.bfloat16
MESH = pl.DeviceIdType.MESH
NT = (((1,), (1,)), ((), ()))

OWN, RIGHT, VERT, DIAG = range(4)


def quadrant_matrix(rowflag):
    out = lax.broadcasted_iota(jnp.int32, (64, 64), 0)
    inn = lax.broadcasted_iota(jnp.int32, (64, 64), 1)
    role = out // 16
    outer = jnp.logical_or(role == OWN, role == DIAG)
    half_i = jnp.where(outer, rowflag, 1 - rowflag)
    half_j = 1 - role % 2
    row = half_i * 4 + (out % 16) // 4
    col = half_j * 4 + out % 4
    return jnp.where(inn == row * 8 + col, 1.0, 0.0)


def head_span(h):
    start = (HD * h) // 128 * 128
    offset = HD * h - start
    return start, offset, (128 if offset + HD <= 128 else 256)


def lane_row(width, low, high):
    lane = lax.broadcasted_iota(jnp.int32, (1, width), 1)
    return jnp.where(jnp.logical_and(lane >= low, lane < high), 1.0, 0.0).astype(BF16)


def layer_scale(x, m0, m1):
    center = jnp.mean(x, -1, keepdims=True)
    moved = x - center
    spread = jnp.mean(moved * moved, -1, keepdims=True)
    return (moved * lax.rsqrt(spread + 1e-6) * (1.0 + m1) + m0).astype(BF16)


def features(label, low):
    lane = lax.broadcasted_iota(jnp.int32, (512, 128), 1) - low
    inside = jnp.logical_and(lane >= 0, lane < 8)
    same = lane == label
    fq = jnp.where(jnp.logical_and(inside, same), 1.0, 0.0)
    fk = jnp.where(jnp.logical_and(inside, jnp.logical_not(same)), -BIG, 0.0)
    return fq.astype(BF16), fk.astype(BF16)


def attend(qkv, base, chunk, fq, fk, mixed):
    def scores(h):
        start, offset, width = head_span(h)
        side = 1 if offset == 0 else 0
        q = qkv[pl.ds(base + chunk * 16, 16), :, start : start + width].reshape(256, width)
        k = qkv[pl.ds(base, 32), :, D + start : D + start + width].reshape(512, width)
        mask = lane_row(width, offset, offset + HD)
        first = mask[:, :128]
        rows = slice(chunk * 256, chunk * 256 + 256)
        q0 = q[:, :128] * first + fq[side, rows]
        k = k * mask
        k0 = k[:, :128] + fk[side]
        if width == 256:
            q0 = jnp.concatenate([q0, q[:, 128:]], axis=1)
            k0 = jnp.concatenate([k0, k[:, 128:]], axis=1)
        return lax.dot_general(q0, k0, NT, preferred_element_type=F32)

    def values(h, s):
        start, offset, width = head_span(h)
        free = 127 if offset == 0 else 0
        s = s - jnp.max(s, axis=1, keepdims=True)
        weights = jnp.exp2(s).astype(BF16)
        v = qkv[pl.ds(base, 32), :, 2 * D + start : 2 * D + start + width].reshape(512, width)
        ones = lane_row(128, free, free + 1)
        v0 = v[:, :128] * (1.0 - ones) + ones
        if width == 256:
            v0 = jnp.concatenate([v0, v[:, 128:]], axis=1)
        out = jnp.dot(weights, v0, preferred_element_type=F32)
        out = out * (1.0 / out[:, free : free + 1])
        head = out[:, :128]
        if offset > 0:
            lane = lax.broadcasted_iota(jnp.int32, (256, 128), 1)
            head = jnp.where(lane >= offset, head, mixed[:, start : start + 128])
        mixed[:, start : start + 128] = head
        if width == 256:
            mixed[:, start + 128 : start + 256] = out[:, 128:]

    held = None
    for h in range(HEADS):
        s = scores(h)
        if held is not None:
            values(h - 1, held)
        held = s
    values(HEADS - 1, held)


def body(
    lat, weights, shard, mod, labels, shift,
    result,
    wbuf, x0, x1, scaled, qkv, rolled, mixed, first, second, feat_q, feat_k, sib, pairs,
    load_sem, sib_send, sib_recv, par_send, par_recv, rel_send, rel_recv,
    out_send, out_recv, back_send, back_recv, own_sem,
):
    ha, wa = lax.axis_index("ha"), lax.axis_index("wa")
    core = wa % 2
    ylo = (wa // 2) % 2
    xx = wa // 4
    chip = wa // 2
    rowflag = 1 - wa % 2
    down = 1 - 2 * (wa % 2)

    def at(h, w):
        return ((h + 8) % 8, (w + 16) % 16)

    sibling = at(ha, wa + 1 - 2 * core)

    def peer(k, sign):
        step = k + 1 if k < 3 else k - 3
        x = (xx + sign * step + 4) % 4
        y = ylo if k < 3 else 1 - ylo
        h = ha if k < 3 else (ha + 4) % 8
        return (h, (x * 2 + y) * 2 + core), x * 2 + y

    send_to = {RIGHT: at(ha, wa - 1), VERT: at(ha - down, wa), DIAG: at(ha + down, wa - 1)}
    back_to = {RIGHT: at(ha, wa + 1), VERT: at(ha + down, wa), DIAG: at(ha + down, wa + 1)}

    loads = []
    for b in range(2):
        for part in range(3):
            cols = pl.ds(part * D, D)
            loads.append(
                pltpu.make_async_copy(
                    weights.at[b, :, cols], wbuf.at[b, :, cols], load_sem.at[b, part]
                )
            )
    for copy in loads:
        copy.start()

    barrier = pltpu.get_barrier_semaphore()
    greet = [sibling] + [peer(k, -1)[0] for k in range(7)]
    greet += list(send_to.values()) + list(back_to.values())
    for device in greet:
        pl.semaphore_signal(barrier, inc=1, device_id=device, device_id_type=MESH)
    pl.semaphore_wait(barrier, len(greet))

    def remote(src, dst, send, recv, device):
        return pltpu.make_async_remote_copy(
            src_ref=src, dst_ref=dst, send_sem=send, recv_sem=recv,
            device_id=device, device_id_type=MESH,
        )

    swap = remote(shard, sib, sib_send, sib_recv, sibling)
    swap.start()

    pick = quadrant_matrix(rowflag).astype(BF16)

    def prepare(f, _):
        x = lat[f].astype(F32).reshape(64, D).astype(BF16)
        x = jnp.dot(pick, x, preferred_element_type=F32)
        y = layer_scale(x, mod[0, 0:1], mod[0, 1:2])
        x = x.astype(BF16)
        base = (f // 8) * 32 + f % 8
        for role in range(4):
            x0[base + role * 8] = x[role * 16 : role * 16 + 16]
            scaled[base + role * 8] = y[role * 16 : role * 16 + 16]
        return 0

    lax.fori_loop(0, 16, prepare, 0)

    swap.wait()
    for b in range(2):
        mine = shard[b].astype(F32)
        theirs = sib[b].astype(F32)
        low = jnp.where(core == 0, mine, theirs).T
        high = jnp.where(core == 0, theirs, mine).T
        pairs[b, chip] = jnp.concatenate([low, high], axis=0).astype(BF16)

    spans = ((0, 80), (80, 64))

    def parts(c, b):
        rows = pl.ds(*spans[c])
        out = []
        for k in range(7):
            device, _ = peer(k, 1)
            ref = pairs.at[b, chip, rows]
            out.append(remote(ref, ref, par_send.at[b, k], par_recv.at[b, k], device))
        return out

    def relays(c, b):
        rows = pl.ds(*spans[c])
        out = []
        for k in range(7):
            _, source = peer(k, -1)
            ref = pairs.at[b, source, rows]
            out.append(remote(ref, ref, rel_send.at[b, k], rel_recv.at[b, k], sibling))
        return out

    for c in range(2):
        @pl.when(core == c)
        def _():
            for b in range(2):
                for copy in parts(c, b):
                    copy.start()

    def pass_on(b):
        for c in range(2):
            @pl.when(core == c)
            def _():
                for copy, forward in zip(parts(c, b), relays(c, b)):
                    copy.wait_recv()
                    forward.start()

    def relayed(b):
        for c in range(2):
            @pl.when(core == c)
            def _():
                for forward in relays(1 - c, b):
                    forward.wait_recv()

    def triples(b, w):
        rows = scaled[pl.ds(w * 32, 32)].reshape(512, D)
        for part in range(3):
            cols = slice(part * D, part * D + D)
            out = jnp.dot(rows, wbuf[b, :, cols], preferred_element_type=F32)
            if part == 0:
                out = out * SCALE
            qkv[pl.ds(w * 32, 32), :, cols] = out.astype(BF16).reshape(32, 16, D)

    def project(b, x):
        w = pairs[b].reshape(D, D)
        branch = lax.dot_general(mixed[...].astype(BF16), w, NT, preferred_element_type=F32)
        return (x.astype(F32) + mod[b, 2:3] * branch).astype(BF16).reshape(16, 16, D)

    for copy in loads[:3]:
        copy.wait()

    def make0(w, _):
        triples(0, w)
        return 0

    lax.fori_loop(0, 2, make0, 0)
    pass_on(0)

    def exchange(w, role):
        place = pl.ds(w * 32 + role * 8, 8)
        return remote(
            first.at[place], x1.at[place], out_send.at[w, role - 1], out_recv.at[w, role - 1],
            send_to[role],
        )

    def block0(w, _):
        base = w * 32
        for side in range(2):
            feat_q[side] = labels[0, side, pl.ds(w * 512, 512)]
            feat_k[side] = labels[1, side, pl.ds(w * 512, 512)]
        for chunk in (1, 0):
            attend(qkv, base, chunk, feat_q, feat_k, mixed)
            if chunk == 1:
                @pl.when(w == 0)
                def _():
                    relayed(0)
            here = pl.ds(base + chunk * 16, 16)
            out = project(0, x0[here].reshape(256, D))
            if chunk == 1:
                first[here] = out
                exchange(w, DIAG).start()
                exchange(w, VERT).start()
            else:
                x1[pl.ds(base, 8)] = out[:8]
                first[pl.ds(base + 8, 8)] = out[8:]
                exchange(w, RIGHT).start()
        return 0

    lax.fori_loop(0, 2, block0, 0)
    pass_on(1)
    for copy in loads[3:]:
        copy.wait()

    def make1(w, _):
        for role in (RIGHT, VERT, DIAG):
            exchange(w, role).wait_recv()

        def norm(t, _):
            place = pl.ds(w * 32 + t * 4, 4)
            x = x1[place].reshape(64, D).astype(F32)
            scaled[place] = layer_scale(x, mod[1, 0:1], mod[1, 1:2]).reshape(4, 16, D)
            return 0

        lax.fori_loop(0, 8, norm, 0)
        triples(1, w)
        return 0

    lax.fori_loop(0, 2, make1, 0)
    relayed(1)

    offset = shift[0]
    row_block = (ha - wa % 2 + 8) % 8
    at_row_end = jnp.where(row_block == 7, 1, 0)
    at_col_end = jnp.where(wa == 15, 1, 0)

    def give_back(w, role):
        place = pl.ds(w * 32 + role * 8, 8)
        return remote(
            second.at[place], result.at[place], back_send.at[w, role - 1],
            back_recv.at[w, role - 1], back_to[role],
        )

    def keep(w):
        place = pl.ds(w * 32, 8)
        return pltpu.make_async_copy(second.at[place], result.at[place], own_sem.at[w])

    def block1(w, _):
        def roll(t, _):
            role, g = t // 8, t % 8
            frame = (w * 8 + g + offset) % 16
            rolled[t] = qkv[(frame // 8) * 32 + role * 8 + frame % 8]
            x0[t] = x1[(frame // 8) * 32 + role * 8 + frame % 8]
            return 0

        lax.fori_loop(0, 32, roll, 0)
        row = lax.broadcasted_iota(jnp.int32, (512, 1), 0)
        role, g = row // 128, (row % 128) // 16
        late = jnp.where(w * 8 + g >= 16 - offset, w, 0)
        far = jnp.where(role >= 2, 1, 0)
        low = (far * rowflag + (1 - far) * (1 - rowflag)) * at_row_end
        side_label = (role % 2) * at_col_end
        label = late * 4 + low * 2 + side_label
        for side in range(2):
            fq, fk = features(label, 120 * side)
            feat_q[side] = fq
            feat_k[side] = fk
        for chunk in (1, 0):
            attend(rolled, 0, chunk, feat_q, feat_k, mixed)
            out = project(1, x0[pl.ds(chunk * 16, 16)].reshape(256, D))
            second[pl.ds(w * 32 + chunk * 16, 16)] = out
            if chunk == 1:
                give_back(w, DIAG).start()
                give_back(w, VERT).start()
            else:
                give_back(w, RIGHT).start()
                keep(w).start()
        return 0

    lax.fori_loop(0, 2, block1, 0)

    for w in range(2):
        keep(w).wait()
        for role in (RIGHT, VERT, DIAG):
            exchange(w, role).wait_send()
            give_back(w, role).wait()
    for c in range(2):
        @pl.when(core == c)
        def _():
            for b in range(2):
                for copy, forward in zip(parts(c, b), relays(c, b)):
                    copy.wait_send()
                    forward.wait_send()


def finish_body(shift, y, out):
    step = pl.program_id(0)
    rowflag = shift[1]
    pick = quadrant_matrix(rowflag).astype(BF16)
    for f in range(4):
        g = (step * 4 + f - shift[0] + 16) % 16
        base = (g // 8) * 32 + g % 8
        rows = jnp.concatenate([y[base + role * 8] for role in range(4)], axis=0)
        x = lax.dot_general(pick, rows, (((0,), (0,)), ((), ())), preferred_element_type=F32)
        out[f] = x.reshape(8, 8, D).astype(BF16)


def local(latent, qkv_weight, proj_weight, modulation, regions, frame_shift):
    wa = lax.axis_index("wa")
    rowflag = 1 - wa % 2

    grid = regions.reshape(2, 8, 2, 4, 2, 4)
    flipped = jnp.where(rowflag == 1, grid, grid[:, :, ::-1])
    order = [(1, 1), (0, 0), (0, 1), (1, 0)]
    label = jnp.stack([flipped[:, :, i, :, j, :] for i, j in order], axis=1).reshape(1024, 1)
    lane = lax.broadcasted_iota(jnp.int32, (2, 1024, 128), 2)
    lane = lane - 120 * lax.broadcasted_iota(jnp.int32, (2, 1024, 128), 0)
    inside = jnp.logical_and(lane >= 0, lane < 8)
    same = lane == label[None]
    fq = jnp.where(jnp.logical_and(inside, same), 1.0, 0.0).astype(BF16)
    fk = jnp.where(jnp.logical_and(inside, jnp.logical_not(same)), -BIG, 0.0).astype(BF16)
    labels = jnp.stack([fq, fk])

    vmem = pl.BlockSpec(memory_space=pltpu.VMEM)
    anywhere = pl.BlockSpec(memory_space=pl.ANY)
    smem = pl.BlockSpec(memory_space=pltpu.SMEM)
    tiles = pltpu.VMEM((64, 16, D), BF16)
    dma = pltpu.SemaphoreType.DMA
    joined = pl.pallas_call(
        body,
        out_shape=jax.ShapeDtypeStruct((64, 16, D), BF16),
        in_specs=[vmem, anywhere, vmem, vmem, vmem, smem],
        out_specs=anywhere,
        scratch_shapes=[
            pltpu.VMEM((2, D, 3 * D), BF16),
            tiles, tiles, tiles,
            pltpu.VMEM((64, 16, 3 * D), BF16),
            pltpu.VMEM((32, 16, 3 * D), BF16),
            pltpu.VMEM((256, D), F32),
            tiles, tiles,
            pltpu.VMEM((2, 512, 128), BF16),
            pltpu.VMEM((2, 512, 128), BF16),
            pltpu.VMEM((2, D, HD), BF16),
            pltpu.VMEM((2, 8, 2 * HD, D), BF16),
            dma((2, 3)),
            dma, dma,
            dma((2, 7)), dma((2, 7)), dma((2, 7)), dma((2, 7)),
            dma((2, 3)), dma((2, 3)), dma((2, 3)), dma((2, 3)),
            dma((2,)),
        ],
        compiler_params=pltpu.CompilerParams(
            collective_id=0, has_side_effects=True, vmem_limit_bytes=62 << 20
        ),
        name="blocks",
    )(latent, qkv_weight, proj_weight, modulation, labels, frame_shift)

    numbers = jnp.stack([frame_shift[0], rowflag.astype(jnp.int32)])
    return pl.pallas_call(
        finish_body,
        out_shape=jax.ShapeDtypeStruct((16, 8, 8, D), BF16),
        grid_spec=pltpu.PrefetchScalarGridSpec(
            num_scalar_prefetch=1,
            grid=(4,),
            in_specs=[pl.BlockSpec((64, 16, D), lambda i, s: (0, 0, 0))],
            out_specs=pl.BlockSpec((4, 8, 8, D), lambda i, s: (i, 0, 0, 0)),
        ),
        compiler_params=pltpu.CompilerParams(vmem_limit_bytes=32 << 20),
        name="finish",
    )(numbers, joined)


def solution(mesh):
    in_specs = (P(None, "ha", "wa", None), P(), P(None, None, "wa"), P(), P(None, "ha", "wa"), P())
    out_specs = P(None, "ha", "wa", None)
    return jax.shard_map(local, mesh=mesh, in_specs=in_specs, out_specs=out_specs, check_vma=False)
```

profile of v0, /device:TPU:4, one launch (start us, length us, event | category | flops | bytes accessed | tf_op | source)
XLA Modules:
  0.0 121.5 jit_solution(9450076518540898450)
XLA Ops:
  0.7 0.1 pad_add_fusion.1.shift
  0.7 1.4 %copy.18.mod = f32[2,3,1152]{2,1,0:T(4,128)} copy(f32[2,3,1152]{2,0,1:T(2,128)} %param.9) | data formatting | bytes 55296 | tf_op args[3]
  2.1 0.9 reshape.45
  2.9 0.3 copy.13
  3.3 0.2 eq.27
  3.5 2.0 %copy.17.shard = bf16[2,1152,72]{2,1,0:T(8,128)(2,1)} copy(bf16[2,1152,72]{1,2,0:T(8,128)(2,1)} %param.8) | data formatting | bytes 663552 | tf_op args[2]
  5.5 0.4 select_convert_fusion.1
  5.9 1.1 pad_maximum_fusion.labels
  7.0 109.5 %blocks.1.y = bf16[64,16,1152]{2,1,0:T(8,128)(2,1)} custom-call(bf16[16,8,8,1152]{3,2,1,0:T(8,128)(2,1)} %lat.1, bf16[2,1152,3456]{2,1,0:T(8,128)(2,1)} %weights.1, bf16[2,1152,72]{2,1,0:T(8,128)(2,1)} %copy.17.shard, f32[2,3,1152]{2,1,0:T(4,128)} %copy.18.mod, bf16[2,2,1024,128]{3,2,1,0:T(8,128)(2,1)} %pad_maximum_fusion.labels, s32[1]{0:T(128)S(6)} %copy.19.shift), custom_call_target="tpu_custom_call" | custom-call | tf_op jit(solution)/shard_map/blocks/pallas_call | solution.py:405
  116.5 0.0 copy-start
  116.5 1.7 %copy-done = bf16[64,16,1152]{2,1,0:T(8,128)(2,1)S(1)} copy-done((bf16[64,16,1152]{2,1,0:T(8,128)(2,1)S(1)}, bf16[64,16,1152]{2,1,0:T(8,128)(2,1)}, u32[]{:S(2)}) %copy-start) | copy-done | bytes 2359320
  118.2 3.3 %finish.1 = bf16[16,8,8,1152]{3,2,1,0:T(8,128)(2,1)} custom-call(s32[2]{0:T(128)S(1)} %pad_add_fusion.1.shift, bf16[64,16,1152]{2,1,0:T(8,128)(2,1)S(1)} %copy-done), custom_call_target="tpu_custom_call" | custom-call | tf_op jit(solution)/shard_map/finish/pallas_call | solution.py:434
  (4 shorter events, 0.1 us)
Async XLA Ops:
  116.5 1.7 %copy-start = (bf16[64,16,1152]{2,1,0:T(8,128)(2,1)S(1)}, bf16[64,16,1152]{2,1,0:T(8,128)(2,1)}, u32[]{:S(2)}) copy-start(bf16[64,16,1152]{2,1,0:T(8,128)(2,1)} %blocks.1.y) | copy-start | bytes 7077892
where the time goes:
time: 122 us; the launch traced here: 121 us
  Pallas kernels  113 us (93%)
  local copies, waits for them, and re-layouts  6.33 us (5%)
  other arithmetic  1.64 us (1%)
    pallas_call x1, Pallas kernels, local(): pl.pallas_call(body, out_shape=jax.ShapeDtypeStruct((64, 16, D), BF16), i...  109 us
    unnamed x4, local copies, waits for them, and re-layouts  5.04 us
    pallas_call x1, Pallas kernels, local(): pl.pallas_call(finish_body, out_shape=jax.ShapeDtypeStruct((16, 8, 8, D),...  3.29 us

commit v1 on v0

v1 whole, which is shorter than its diff:
```python
import functools
import math

import jax
import jax.numpy as jnp
from jax import lax
from jax.experimental import pallas as pl
from jax.experimental.pallas import tpu as pltpu
from jax.sharding import PartitionSpec as P

D = 1152
HEADS = 16
HD = 72
BIG = 1e30
SCALE = math.log2(math.e) / math.sqrt(HD)
F32 = jnp.float32
BF16 = jnp.bfloat16
MESH = pl.DeviceIdType.MESH
NT = (((1,), (1,)), ((), ()))

OWN, RIGHT, VERT, DIAG = range(4)


def quadrant_matrix(rowflag, leftflag):
    out = lax.broadcasted_iota(jnp.int32, (64, 64), 0)
    inn = lax.broadcasted_iota(jnp.int32, (64, 64), 1)
    role = out // 16
    half_j = 1 - role % 2
    flag = jnp.where(half_j == 1, rowflag, leftflag)
    half_i = jnp.where(role < 2, flag, 1 - flag)
    row = half_i * 4 + (out % 16) // 4
    col = half_j * 4 + out % 4
    return jnp.where(inn == row * 8 + col, 1.0, 0.0)


def head_span(h):
    start = (HD * h) // 128 * 128
    offset = HD * h - start
    return start, offset, (128 if offset + HD <= 128 else 256)


def lane_row(width, low, high):
    lane = lax.broadcasted_iota(jnp.int32, (1, width), 1)
    return jnp.where(jnp.logical_and(lane >= low, lane < high), 1.0, 0.0).astype(BF16)


def layer_scale(x, m0, m1):
    center = jnp.mean(x, -1, keepdims=True)
    moved = x - center
    spread = jnp.mean(moved * moved, -1, keepdims=True)
    return (moved * lax.rsqrt(spread + 1e-6) * (1.0 + m1) + m0).astype(BF16)


def features(label, rows):
    lane = lax.broadcasted_iota(jnp.int32, (rows, 128), 1)
    out = []
    for low in (0, 120):
        inside = jnp.logical_and(lane >= low, lane < low + 8)
        same = lane - low == label
        fq = jnp.where(jnp.logical_and(inside, same), 1.0, 0.0)
        fk = jnp.where(jnp.logical_and(inside, jnp.logical_not(same)), -BIG, 0.0)
        out.append((fq.astype(BF16), fk.astype(BF16)))
    return out


def attend(qkv, base, chunk, fq, fk, mixed):
    def scores(h):
        start, offset, width = head_span(h)
        side = 1 if offset == 0 else 0
        q = qkv[pl.ds(base + chunk * 16, 16), :, start : start + width].reshape(256, width)
        k = qkv[pl.ds(base, 32), :, D + start : D + start + width].reshape(512, width)
        mask = lane_row(width, offset, offset + HD)
        first = mask[:, :128]
        q0 = q[:, :128] * first + fq[side, pl.ds(base + chunk * 16, 16)].reshape(256, 128)
        k = k * mask
        k0 = k[:, :128] + fk[side, pl.ds(base, 32)].reshape(512, 128)
        if width == 256:
            q0 = jnp.concatenate([q0, q[:, 128:]], axis=1)
            k0 = jnp.concatenate([k0, k[:, 128:]], axis=1)
        return lax.dot_general(q0, k0, NT, preferred_element_type=F32)

    def values(h, s):
        start, offset, width = head_span(h)
        free = 127 if offset == 0 else 0
        s = s - jnp.max(s, axis=1, keepdims=True)
        weights = jnp.exp2(s).astype(BF16)
        v = qkv[pl.ds(base, 32), :, 2 * D + start : 2 * D + start + width].reshape(512, width)
        ones = lane_row(128, free, free + 1)
        v0 = v[:, :128] * (1.0 - ones) + ones
        if width == 256:
            v0 = jnp.concatenate([v0, v[:, 128:]], axis=1)
        out = jnp.dot(weights, v0, preferred_element_type=F32)
        out = out * (1.0 / out[:, free : free + 1])
        head = out[:, :128]
        if offset > 0:
            lane = lax.broadcasted_iota(jnp.int32, (256, 128), 1)
            head = jnp.where(lane >= offset, head, mixed[:, start : start + 128])
        mixed[:, start : start + 128] = head
        if width == 256:
            mixed[:, start + 128 : start + 256] = out[:, 128:]

    held = None
    for h in range(HEADS):
        s = scores(h)
        if held is not None:
            values(h - 1, held)
        held = s
    values(HEADS - 1, held)


def body(
    lat, weights, shard, mod, regions, shift,
    result,
    wbuf, x0, x1, scaled, qkv, rolled, mixed, first, second, back, final, feat_q, feat_k,
    mine, sib, pairs,
    load_sem, sib_send, sib_recv, x_send, x_recv, flip_send, flip_recv, rel_send, rel_recv,
    out_send, out_recv, back_send, back_recv, end_sem,
):
    ha, wa = lax.axis_index("ha"), lax.axis_index("wa")
    core = wa % 2
    ylo = (wa // 2) % 2
    xx = wa // 4
    chip = wa // 2
    rowflag = 1 - (core + ylo) % 2
    leftflag = core * (1 - rowflag) + (1 - core) * rowflag
    step = 2 * rowflag - 1
    leftstep = 2 * leftflag - 1

    def at(h, w):
        return ((h + 8) % 8, (w + 16) % 16)

    sibling = at(ha, wa + 1 - 2 * core)
    across = [
        ((ha + 4 * far) % 8, (xx * 2 + 1 - ylo) * 2 + core) for far in (core, 1)
    ]

    def along(k):
        x = (xx + k + 5) % 4
        return (ha, (x * 2 + ylo) * 2 + core), x * 2 + ylo

    send_to = {RIGHT: at(ha, wa - 1), VERT: at(ha - step, wa), DIAG: at(ha - leftstep, wa - 1)}
    back_to = {RIGHT: at(ha, wa + 1), VERT: at(ha + step, wa), DIAG: at(ha + step, wa + 1)}

    def loads(b):
        out = []
        for part in range(3):
            cols = pl.ds(part * D, D)
            out.append(
                pltpu.make_async_copy(weights.at[b, :, cols], wbuf.at[:, cols], load_sem.at[b, part])
            )
        return out

    for copy in loads(0):
        copy.start()

    barrier = pltpu.get_barrier_semaphore()
    greet = [sibling] + across + [along(k)[0] for k in range(3)]
    greet += list(send_to.values()) + list(back_to.values())
    for device in greet:
        pl.semaphore_signal(barrier, inc=1, device_id=device, device_id_type=MESH)
    pl.semaphore_wait(barrier, len(greet))

    def remote(src, dst, send, recv, device):
        return pltpu.make_async_remote_copy(
            src_ref=src, dst_ref=dst, send_sem=send, recv_sem=recv,
            device_id=device, device_id_type=MESH,
        )

    pad = jnp.zeros((8, D), F32)
    for b in range(2):
        mine[b] = jnp.concatenate([shard[b].astype(F32), pad], axis=0).astype(BF16)
    swap = remote(mine, sib, sib_send, sib_recv, sibling)
    swap.start()

    pick = quadrant_matrix(rowflag, leftflag).astype(BF16)
    places = jnp.dot(
        pick, regions[...].reshape(64, 16).astype(F32).astype(BF16), preferred_element_type=F32
    ).astype(jnp.int32)

    def prepare_frame(f):
        x = lat[f].astype(F32).reshape(64, D).astype(BF16)
        x = jnp.dot(pick, x, preferred_element_type=F32)
        y = layer_scale(x, mod[0, 0:1], mod[1, 0:1])
        x = x.astype(BF16)
        frame = lax.broadcasted_iota(jnp.int32, (64, 16), 1)
        label = jnp.sum(jnp.where(frame == f, places, 0), axis=1, keepdims=True)
        feats = features(label, 64)
        base = (f // 8) * 32 + f % 8
        for role in range(4):
            rows = slice(role * 16, role * 16 + 16)
            x0[base + role * 8] = x[rows]
            scaled[base + role * 8] = y[rows]
            for side in range(2):
                feat_q[side, base + role * 8] = feats[side][0][rows]
                feat_k[side, base + role * 8] = feats[side][1][rows]

    def prepare(i, _):
        prepare_frame(2 * i)
        prepare_frame(2 * i + 1)
        return 0

    lax.fori_loop(0, 3, prepare, 0)

    swap.wait()
    for b in range(2):
        own = mine[b].astype(F32)[:HD]
        theirs = sib[b].astype(F32)[:HD]
        low = jnp.where(core == 0, own, theirs)
        high = jnp.where(core == 0, theirs, own)
        pairs[b, chip] = jnp.concatenate([low, high], axis=0).astype(BF16)

    spans = ((0, 80), (80, 64))

    def x_copies(c, b):
        ref = pairs.at[b, chip, pl.ds(*spans[c])]
        return [
            remote(ref, ref, x_send.at[b, k], x_recv.at[b, k], along(k)[0]) for k in range(3)
        ]

    def row_chips(y):
        return [xx * 2 + y] + [((xx - k + 3) % 4) * 2 + y for k in range(3)]

    def flip_copies(c, b):
        out = []
        for k, source in enumerate(row_chips(ylo)):
            ref = pairs.at[b, source, pl.ds(*spans[c])]
            out.append(remote(ref, ref, flip_send.at[b, k], flip_recv.at[b, k], across[b]))
        return out

    def relay_copies(c, b):
        out = []
        for k, source in enumerate(row_chips(ylo)[1:] + row_chips(1 - ylo)):
            ref = pairs.at[b, source, pl.ds(*spans[c])]
            out.append(remote(ref, ref, rel_send.at[b, k], rel_recv.at[b, k], sibling))
        return out

    def by_core(act):
        for c in range(2):
            @pl.when(core == c)
            def _():
                act(c)

    def gather_start(b):
        def act(c):
            flip_copies(c, b)[0].start()
            for copy in x_copies(c, b):
                copy.start()
        by_core(act)

    def gather_turn(b):
        def act(c):
            flips, relays = flip_copies(c, b)[1:], relay_copies(c, b)[:3]
            for copy, flip, relay in zip(x_copies(c, b), flips, relays):
                copy.wait_recv()
                flip.start()
                relay.start()
        by_core(act)

    def gather_relay(b):
        def act(c):
            for flip, relay in zip(flip_copies(c, b), relay_copies(c, b)[3:]):
                flip.wait_recv()
                relay.start()
        by_core(act)

    def gather_end(b):
        def act(c):
            for relay in relay_copies(1 - c, b):
                relay.wait_recv()
        by_core(act)

    gather_start(0)
    lax.fori_loop(3, 8, prepare, 0)

    def triple(place, count, part):
        rows = scaled[place].reshape(count * 16, D)
        cols = pl.ds(pl.multiple_of(part * D, 128), D)
        out = jnp.dot(rows, wbuf[:, cols], preferred_element_type=F32)
        out = out * jnp.where(part == 0, SCALE, 1.0)
        qkv[place, :, cols] = out.astype(BF16).reshape(count, 16, D)

    def project(b, x, w):
        weight = pairs[b].reshape(D, D)
        branch = lax.dot_general(mixed[w].astype(BF16), weight, NT, preferred_element_type=F32)
        return (x.astype(F32) + mod[2, b : b + 1] * branch).astype(BF16).reshape(16, 16, D)

    for copy in loads(0):
        copy.wait()

    def make0(i, _):
        triple(pl.ds((i // 3) * 32, 32), 32, i % 3)
        return 0

    lax.fori_loop(0, 4, make0, 0)
    gather_turn(0)
    gather_start(1)
    lax.fori_loop(4, 6, make0, 0)
    for copy in loads(1):
        copy.start()

    def exchange(w, role):
        place = pl.ds(w * 32 + role * 8, 8)
        return remote(
            first.at[place], x1.at[place], out_send.at[w, role - 1], out_recv.at[w, role - 1],
            send_to[role],
        )

    def ahead(w, _):
        attend(qkv, w * 32, 1, feat_q, feat_k, mixed.at[w])

        @pl.when(w == 0)
        def _():
            gather_relay(0)
        return 0

    lax.fori_loop(0, 2, ahead, 0)
    gather_turn(1)
    gather_end(0)

    def far_pieces(w, _):
        here = pl.ds(w * 32 + 16, 16)
        first[here] = project(0, x0[here].reshape(256, D), w)
        exchange(w, DIAG).start()
        exchange(w, VERT).start()
        return 0

    lax.fori_loop(0, 2, far_pieces, 0)

    def near_pieces(w, _):
        base = w * 32
        attend(qkv, base, 0, feat_q, feat_k, mixed.at[w])
        out = project(0, x0[pl.ds(base, 16)].reshape(256, D), w)
        x1[pl.ds(base, 8)] = out[:8]
        first[pl.ds(base + 8, 8)] = out[8:]
        exchange(w, RIGHT).start()
        return 0

    lax.fori_loop(0, 2, near_pieces, 0)

    offset = shift[0]
    row_block = (ha + rowflag + 7) % 8
    at_row_end = jnp.where(row_block == 7, 1, 0)
    at_col_end = jnp.where(wa == 15, 1, 0)

    def label_tiles(i, _):
        w, role = i // 4, i % 4
        frame = w * 8 + lax.broadcasted_iota(jnp.int32, (128, 1), 0) // 16
        late = jnp.where(frame >= 16 - offset, w, 0)
        far = role // 2
        low = (far * rowflag + (1 - far) * (1 - rowflag)) * at_row_end
        feats = features(late * 4 + low * 2 + (role % 2) * at_col_end, 128)
        for side in range(2):
            feat_q[side, pl.ds(i * 8, 8)] = feats[side][0].reshape(8, 16, 128)
            feat_k[side, pl.ds(i * 8, 8)] = feats[side][1].reshape(8, 16, 128)
        return 0

    lax.fori_loop(0, 8, label_tiles, 0)

    for copy in loads(1):
        copy.wait()

    def norm(t, _):
        for k in range(2):
            place = pl.ds(t * 8 + k * 4, 4)
            x = x1[place].reshape(64, D).astype(F32)
            scaled[place] = layer_scale(x, mod[0, 1:2], mod[1, 1:2]).reshape(4, 16, D)
        return 0

    for chunk in (1, 0):
        def make1(w, _):
            for role in ((VERT, DIAG) if chunk == 1 else (RIGHT,)):
                exchange(w, role).wait_recv()
            start = w * 32 + chunk * 16
            lax.fori_loop(start // 8, start // 8 + 2, norm, 0)

            def part(p, _):
                triple(pl.ds(start, 16), 16, p)
                return 0

            lax.fori_loop(0, 3, part, 0)
            return 0

        lax.fori_loop(0, 2, make1, 0)
        if chunk == 1:
            gather_relay(1)

    def give_back(w, role):
        place = pl.ds(w * 32 + role * 8, 8)
        return remote(
            second.at[place], back.at[place], back_send.at[w, role - 1],
            back_recv.at[w, role - 1], back_to[role],
        )

    def roll(i, _):
        w, role = i // 4, i % 4
        for g in range(8):
            frame = (w * 8 + g + offset) % 16
            source = (frame // 8) * 32 + role * 8 + frame % 8
            rolled[i * 8 + g] = qkv[source]
            x0[i * 8 + g] = x1[source]
        return 0

    lax.fori_loop(0, 8, roll, 0)

    for chunk in (1, 0):
        def block1(w, _):
            base = w * 32
            attend(rolled, base, chunk, feat_q, feat_k, mixed.at[w])
            here = pl.ds(base + chunk * 16, 16)
            if chunk == 1:
                @pl.when(w == 0)
                def _():
                    gather_end(1)
            second[here] = project(1, x0[here].reshape(256, D), w)
            if chunk == 1:
                give_back(w, DIAG).start()
                give_back(w, VERT).start()
            else:
                give_back(w, RIGHT).start()
            return 0

        lax.fori_loop(0, 2, block1, 0)

    for w in range(2):
        for role in (RIGHT, VERT, DIAG):
            give_back(w, role).wait_recv()

    def last(i):
        return pltpu.make_async_copy(
            final.at[pl.ds(i * 4, 4)], result.at[pl.ds(i * 4, 4)], end_sem.at[i]
        )

    def restore(i, _):
        for k in range(4):
            g = (i * 4 + k - offset + 16) % 16
            base = (g // 8) * 32 + g % 8
            rows = [second[base]] + [back[base + role * 8] for role in (RIGHT, VERT, DIAG)]
            x = lax.dot_general(
                pick, jnp.concatenate(rows, axis=0), (((0,), (0,)), ((), ())),
                preferred_element_type=F32,
            )
            final[i * 4 + k] = x.reshape(8, 8, D).astype(BF16)
        last(i).start()
        return 0

    lax.fori_loop(0, 4, restore, 0)

    for w in range(2):
        for role in (RIGHT, VERT, DIAG):
            exchange(w, role).wait_send()
            give_back(w, role).wait_send()

    def act(c):
        for b in range(2):
            for copy in x_copies(c, b) + flip_copies(c, b) + relay_copies(c, b):
                copy.wait_send()

    by_core(act)
    for i in range(4):
        last(i).wait()


def local(latent, qkv_weight, proj_weight, modulation, regions, frame_shift):
    vmem = pl.BlockSpec(memory_space=pltpu.VMEM)
    anywhere = pl.BlockSpec(memory_space=pl.ANY)
    smem = pl.BlockSpec(memory_space=pltpu.SMEM)
    tiles = pltpu.VMEM((64, 16, D), BF16)
    triples = pltpu.VMEM((64, 16, 3 * D), BF16)
    feats = pltpu.VMEM((2, 64, 16, 128), BF16)
    shards = pltpu.VMEM((2, 80, D), BF16)
    dma = pltpu.SemaphoreType.DMA
    return pl.pallas_call(
        body,
        out_shape=jax.ShapeDtypeStruct((16, 8, 8, D), BF16),
        in_specs=[vmem, anywhere, vmem, vmem, vmem, smem],
        out_specs=anywhere,
        scratch_shapes=[
            pltpu.VMEM((D, 3 * D), BF16),
            tiles, tiles, tiles,
            triples, triples,
            pltpu.VMEM((2, 256, D), F32),
            tiles, tiles, tiles,
            pltpu.VMEM((16, 8, 8, D), BF16),
            feats, feats,
            shards, shards,
            pltpu.VMEM((2, 8, 2 * HD, D), BF16),
            dma((2, 3)),
            dma, dma,
            dma((2, 3)), dma((2, 3)), dma((2, 4)), dma((2, 4)), dma((2, 7)), dma((2, 7)),
            dma((2, 3)), dma((2, 3)), dma((2, 3)), dma((2, 3)),
            dma((4,)),
        ],
        compiler_params=pltpu.CompilerParams(
            collective_id=0, has_side_effects=True, vmem_limit_bytes=62 << 20
        ),
        name="blocks",
    )(
        latent,
        qkv_weight,
        jnp.swapaxes(proj_weight, 1, 2),
        jnp.swapaxes(modulation, 0, 1),
        jnp.transpose(regions, (1, 2, 0)),
        frame_shift,
    )


def solution(mesh):
    in_specs = (P(None, "ha", "wa", None), P(), P(None, None, "wa"), P(), P(None, "ha", "wa"), P())
    out_specs = P(None, "ha", "wa", None)
    return jax.shard_map(local, mesh=mesh, in_specs=in_specs, out_specs=out_specs, check_vma=False)
```

time: 122 us -> 103 us (0.84)
  the two profiles are of different devices: /device:TPU:4 before, /device:TPU:104 now
where the time goes in v1:
time: 103 us
  Pallas kernels  99.1 us (96%)
  local copies, waits for them, and re-layouts  3.26 us (3%)
    pallas_call x1, Pallas kernels, local(): pl.pallas_call(body, out_shape=jax.ShapeDtypeStruct((16, 8, 8, D), BF16),...  99.1 us
    unnamed x1, local copies, waits for them, and re-layouts  3.26 us

profile of v1, /device:TPU:104, one launch (start us, length us, event | category | flops | bytes accessed | tf_op | source)
XLA Modules:
  0.0 103.0 jit_solution(16805210898931762731)
XLA Ops:
  0.7 99.1 %blocks.1 = bf16[16,8,8,1152]{3,2,1,0:T(8,128)(2,1)} custom-call(bf16[16,8,8,1152]{3,2,1,0:T(8,128)(2,1)} %lat.1, bf16[2,1152,3456]{2,1,0:T(8,128)(2,1)} %weights.1, bf16[2,72,1152]{2,1,0:T(8,128)(2,1)} %bitcast.3, f32[3,2,1152]{2,1,0:T(2,128)} %bitcast.5, s32[8,8,16]{2,1,0:T(8,128)} %bitcast.4, s32[1]{0:T(128)S(6)} %copy.8.shift), custom_call_target="tpu_custom_call" | custom-call | tf_op jit(solution)/shard_map/blocks/pallas_call | solution.py:472
  99.7 3.3 %copy.9 = bf16[16,8,8,1152]{3,2,1,0:T(8,128)(2,1)} copy(bf16[16,8,8,1152]{3,2,1,0:T(8,128)(2,1)} %blocks.1) | data formatting | bytes 4718592

commit v2 on v1

--- a/solution.py
+++ b/solution.py
@@ -19,6 +19,12 @@
 NT = (((1,), (1,)), ((), ()))
 
 OWN, RIGHT, VERT, DIAG = range(4)
+
+
+def corner_flags(wa):
+    core, ylo = wa % 2, (wa // 2) % 2
+    rowflag = 1 - (core + ylo) % 2
+    return rowflag, core * (1 - rowflag) + (1 - core) * rowflag
 
 
 def quadrant_matrix(rowflag, leftflag):
@@ -111,18 +117,18 @@
 def body(
     lat, weights, shard, mod, regions, shift,
     result,
-    wbuf, x0, x1, scaled, qkv, rolled, mixed, first, second, back, final, feat_q, feat_k,
+    wbuf, x0, x1, scaled, qkv, rolled, mixed, first, second, passed, feat_q, feat_k,
     mine, sib, pairs,
     load_sem, sib_send, sib_recv, x_send, x_recv, flip_send, flip_recv, rel_send, rel_recv,
-    out_send, out_recv, back_send, back_recv, end_sem,
+    out_send, out_recv, back_send, back_recv, pass_send, pass_recv, own_sem,
 ):
     ha, wa = lax.axis_index("ha"), lax.axis_index("wa")
     core = wa % 2
     ylo = (wa // 2) % 2
     xx = wa // 4
     chip = wa // 2
-    rowflag = 1 - (core + ylo) % 2
-    leftflag = core * (1 - rowflag) + (1 - core) * rowflag
+    depth = ha % 4
+    rowflag, leftflag = corner_flags(wa)
     step = 2 * rowflag - 1
     leftstep = 2 * leftflag - 1
 
@@ -366,7 +372,7 @@
             scaled[place] = layer_scale(x, mod[0, 1:2], mod[1, 1:2]).reshape(4, 16, D)
         return 0
 
-    for chunk in (1, 0):
+    for chunk in (0, 1):
         def make1(w, _):
             for role in ((VERT, DIAG) if chunk == 1 else (RIGHT,)):
                 exchange(w, role).wait_recv()
@@ -381,15 +387,35 @@
             return 0
 
         lax.fori_loop(0, 2, make1, 0)
-        if chunk == 1:
+        if chunk == 0:
             gather_relay(1)
+
+    by_z = core * jnp.where(depth == 3, 1 - rowflag, jnp.where(depth == 0, rowflag, 0))
+    passes = core * jnp.where(depth == 2, 1 - rowflag, jnp.where(depth == 1, rowflag, 0))
 
     def give_back(w, role):
         place = pl.ds(w * 32 + role * 8, 8)
         return remote(
-            second.at[place], back.at[place], back_send.at[w, role - 1],
+            second.at[place], result.at[place], back_send.at[w, role - 1],
             back_recv.at[w, role - 1], back_to[role],
         )
+
+    def by_neighbour(w):
+        place = pl.ds(w * 32 + DIAG * 8, 8)
+        return remote(
+            second.at[place], passed.at[w], pass_send.at[w], pass_recv.at[w], back_to[VERT]
+        )
+
+    def pass_back(w):
+        place = pl.ds(w * 32 + DIAG * 8, 8)
+        return remote(
+            passed.at[w], result.at[place], pass_send.at[w], back_recv.at[w, DIAG - 1],
+            back_to[RIGHT],
+        )
+
+    def keep(w):
+        place = pl.ds(w * 32, 8)
+        return pltpu.make_async_copy(second.at[place], result.at[place], own_sem.at[w])
 
     def roll(i, _):
         w, role = i // 4, i % 4
@@ -413,42 +439,45 @@
                     gather_end(1)
             second[here] = project(1, x0[here].reshape(256, D), w)
             if chunk == 1:
-                give_back(w, DIAG).start()
                 give_back(w, VERT).start()
+
+                @pl.when(by_z == 1)
+                def _():
+                    by_neighbour(w).start()
+
+                @pl.when(by_z == 0)
+                def _():
+                    give_back(w, DIAG).start()
             else:
                 give_back(w, RIGHT).start()
+                keep(w).start()
             return 0
 
         lax.fori_loop(0, 2, block1, 0)
 
+    @pl.when(passes == 1)
+    def _():
+        for w in range(2):
+            by_neighbour(w).wait_recv()
+            pass_back(w).start()
+        for w in range(2):
+            pass_back(w).wait_send()
+
     for w in range(2):
-        for role in (RIGHT, VERT, DIAG):
-            give_back(w, role).wait_recv()
-
-    def last(i):
-        return pltpu.make_async_copy(
-            final.at[pl.ds(i * 4, 4)], result.at[pl.ds(i * 4, 4)], end_sem.at[i]
-        )
-
-    def restore(i, _):
-        for k in range(4):
-            g = (i * 4 + k - offset + 16) % 16
-            base = (g // 8) * 32 + g % 8
-            rows = [second[base]] + [back[base + role * 8] for role in (RIGHT, VERT, DIAG)]
-            x = lax.dot_general(
-                pick, jnp.concatenate(rows, axis=0), (((0,), (0,)), ((), ())),
-                preferred_element_type=F32,
-            )
-            final[i * 4 + k] = x.reshape(8, 8, D).astype(BF16)
-        last(i).start()
-        return 0
-
-    lax.fori_loop(0, 4, restore, 0)
-
-    for w in range(2):
+        keep(w).wait()
         for role in (RIGHT, VERT, DIAG):
             exchange(w, role).wait_send()
+            give_back(w, role).wait_recv()
+        for role in (RIGHT, VERT):
             give_back(w, role).wait_send()
+
+        @pl.when(by_z == 1)
+        def _():
+            by_neighbour(w).wait_send()
+
+        @pl.when(by_z == 0)
+        def _():
+            give_back(w, DIAG).wait_send()
 
     def act(c):
         for b in range(2):
@@ -456,8 +485,36 @@
                 copy.wait_send()
 
     by_core(act)
-    for i in range(4):
-        last(i).wait()
+
+
+def finish_body(shift, joined, out, tiles, final, in_sem, out_sem):
+    back = quadrant_matrix(*corner_flags(lax.axis_index("wa"))).T.astype(BF16)
+
+    def load(w, role):
+        place = pl.ds(w * 32 + role * 8, 8)
+        return pltpu.make_async_copy(joined.at[place], tiles.at[place], in_sem.at[w, role])
+
+    for w in range(2):
+        for role in range(4):
+            load(w, role).start()
+
+    def store(t):
+        frame = (t + shift[0]) % 16
+        return pltpu.make_async_copy(final.at[t], out.at[frame], out_sem.at[t])
+
+    for w in range(2):
+        for role in range(4):
+            load(w, role).wait()
+
+        for t in range(w * 8, w * 8 + 8):
+            base = w * 32 + t % 8
+            rows = jnp.concatenate([tiles[base + role * 8] for role in range(4)], axis=0)
+            x = jnp.dot(back, rows, preferred_element_type=F32)
+            final[t] = x.reshape(8, 8, D).astype(BF16)
+            store(t).start()
+
+    for t in range(16):
+        store(t).wait()
 
 
 def local(latent, qkv_weight, proj_weight, modulation, regions, frame_shift):
@@ -469,9 +526,9 @@
     feats = pltpu.VMEM((2, 64, 16, 128), BF16)
     shards = pltpu.VMEM((2, 80, D), BF16)
     dma = pltpu.SemaphoreType.DMA
-    return pl.pallas_call(
+    joined = pl.pallas_call(
         body,
-        out_shape=jax.ShapeDtypeStruct((16, 8, 8, D), BF16),
+        out_shape=jax.ShapeDtypeStruct((64, 16, D), BF16),
         in_specs=[vmem, anywhere, vmem, vmem, vmem, smem],
         out_specs=anywhere,
         scratch_shapes=[
@@ -479,8 +536,8 @@
             tiles, tiles, tiles,
             triples, triples,
             pltpu.VMEM((2, 256, D), F32),
-            tiles, tiles, tiles,
-            pltpu.VMEM((16, 8, 8, D), BF16),
+            tiles, tiles,
+            pltpu.VMEM((2, 8, 16, D), BF16),
             feats, feats,
             shards, shards,
             pltpu.VMEM((2, 8, 2 * HD, D), BF16),
@@ -488,7 +545,7 @@
             dma, dma,
             dma((2, 3)), dma((2, 3)), dma((2, 4)), dma((2, 4)), dma((2, 7)), dma((2, 7)),
             dma((2, 3)), dma((2, 3)), dma((2, 3)), dma((2, 3)),
-            dma((4,)),
+            dma((2,)), dma((2,)), dma((2,)),
         ],
         compiler_params=pltpu.CompilerParams(
             collective_id=0, has_side_effects=True, vmem_limit_bytes=62 << 20
@@ -502,6 +559,15 @@
         jnp.transpose(regions, (1, 2, 0)),
         frame_shift,
     )
+    return pl.pallas_call(
+        finish_body,
+        out_shape=jax.ShapeDtypeStruct((16, 8, 8, D), BF16),
+        in_specs=[smem, anywhere],
+        out_specs=anywhere,
+        scratch_shapes=[tiles, pltpu.VMEM((16, 8, 8, D), BF16), dma((2, 4)), dma((16,))],
+        compiler_params=pltpu.CompilerParams(vmem_limit_bytes=62 << 20),
+        name="finish",
+    )(frame_shift, joined)
 
 
 def solution(mesh):

time: 103 us -> 96.6 us (0.938)
  the two profiles are of different devices: /device:TPU:104 before, /device:TPU:17 now
where the time goes in v2:
time: 96.6 us; the launch traced here: 96.4 us
  Pallas kernels  95.6 us (99%)
    pallas_call x1, Pallas kernels, local(): pl.pallas_call(body, out_shape=jax.ShapeDtypeStruct((64, 16, D), BF16), i...  92.5 us
    pallas_call x1, Pallas kernels, local(): pl.pallas_call(finish_body, out_shape=jax.ShapeDtypeStruct((16, 8, 8, D),...  3.1 us

profile of v2, /device:TPU:17, one launch (start us, length us, event | category | flops | bytes accessed | tf_op | source)
XLA Modules:
  0.0 96.4 jit_solution(5453037593596602114)
XLA Ops:
  0.7 92.5 %blocks.1.joined = bf16[64,16,1152]{2,1,0:T(8,128)(2,1)} custom-call(bf16[16,8,8,1152]{3,2,1,0:T(8,128)(2,1)} %lat.1, bf16[2,1152,3456]{2,1,0:T(8,128)(2,1)} %weights.1, bf16[2,72,1152]{2,1,0:T(8,128)(2,1)} %bitcast.3, f32[3,2,1152]{2,1,0:T(2,128)} %bitcast.5, s32[8,8,16]{2,1,0:T(8,128)} %bitcast.4, s32[1]{0:T(128)S(6)} %copy.7.shift), custom_call_target="tpu_custom_call" | custom-call | tf_op jit(solution)/shard_map/blocks/pallas_call | solution.py:529
  93.2 3.1 %finish.1 = bf16[16,8,8,1152]{3,2,1,0:T(8,128)(2,1)} custom-call(s32[1]{0:T(128)S(6)} %copy.7.shift, bf16[64,16,1152]{2,1,0:T(8,128)(2,1)} %blocks.1.joined), custom_call_target="tpu_custom_call" | custom-call | tf_op jit(solution)/shard_map/finish/pallas_call | solution.py:562

commit v3 on v2

--- a/solution.py
+++ b/solution.py
@@ -105,13 +105,11 @@
         if width == 256:
             mixed[:, start + 128 : start + 256] = out[:, 128:]
 
-    held = None
+    held = [scores(0), scores(1)]
     for h in range(HEADS):
-        s = scores(h)
-        if held is not None:
-            values(h - 1, held)
-        held = s
-    values(HEADS - 1, held)
+        if h + 2 < HEADS:
+            held.append(scores(h + 2))
+        values(h, held.pop(0))
 
 
 def body(
@@ -323,11 +321,16 @@
     gather_turn(1)
     gather_end(0)
 
+    later = (1 - core) * jnp.where(depth == 0, 1 - rowflag, jnp.where(depth == 3, rowflag, 0))
+
     def far_pieces(w, _):
         here = pl.ds(w * 32 + 16, 16)
         first[here] = project(0, x0[here].reshape(256, D), w)
-        exchange(w, DIAG).start()
         exchange(w, VERT).start()
+
+        @pl.when(later == 0)
+        def _():
+            exchange(w, DIAG).start()
         return 0
 
     lax.fori_loop(0, 2, far_pieces, 0)
@@ -342,6 +345,11 @@
         return 0
 
     lax.fori_loop(0, 2, near_pieces, 0)
+
+    @pl.when(later == 1)
+    def _():
+        for w in range(2):
+            exchange(w, DIAG).start()
 
     offset = shift[0]
     row_block = (ha + rowflag + 7) % 8

time: 96.6 us -> 96.6 us (level)
  no operation moved by 1% of the time
where the time goes in v3:
time: 96.6 us; the launch traced here: 96.4 us
  Pallas kernels  95.6 us (99%)
    pallas_call x1, Pallas kernels, local(): pl.pallas_call(body, out_shape=jax.ShapeDtypeStruct((64, 16, D), BF16), i...  92.5 us
    pallas_call x1, Pallas kernels, local(): pl.pallas_call(finish_body, out_shape=jax.ShapeDtypeStruct((16, 8, 8, D),...  3.09 us

profile of v3, /device:TPU:17, one launch (start us, length us, event | category | flops | bytes accessed | tf_op | source)
XLA Modules:
  0.0 96.4 jit_solution(12233942086522296534)
XLA Ops:
  0.7 92.5 %blocks.1.joined = bf16[64,16,1152]{2,1,0:T(8,128)(2,1)} custom-call(bf16[16,8,8,1152]{3,2,1,0:T(8,128)(2,1)} %lat.1, bf16[2,1152,3456]{2,1,0:T(8,128)(2,1)} %weights.1, bf16[2,72,1152]{2,1,0:T(8,128)(2,1)} %bitcast.3, f32[3,2,1152]{2,1,0:T(2,128)} %bitcast.5, s32[8,8,16]{2,1,0:T(8,128)} %bitcast.4, s32[1]{0:T(128)S(6)} %copy.7.shift), custom_call_target="tpu_custom_call" | custom-call | tf_op jit(solution)/shard_map/blocks/pallas_call | solution.py:537
  93.1 3.1 %finish.1 = bf16[16,8,8,1152]{3,2,1,0:T(8,128)(2,1)} custom-call(s32[1]{0:T(128)S(6)} %copy.7.shift, bf16[64,16,1152]{2,1,0:T(8,128)(2,1)} %blocks.1.joined), custom_call_target="tpu_custom_call" | custom-call | tf_op jit(solution)/shard_map/finish/pallas_call | solution.py:570
